TPU v7x, 768 devices: a whole 4x8x12 slice. The times are simulated.
768 devices in a mesh: dom: 192 (over y, z, core), grp: 4 (over x).
Axes of the slice: x: 4, y: 8, z: 12, core: 2. Of those that a mesh axis runs over, the one named last changes fastest.
Arguments:
- trace: float32 [192, 4, 72, 1280], P('dom', 'grp'), may hold values from -6 to 6
- rhs: float32 [192, 4, 72, 1280], P('dom', 'grp'), may hold values from -6 to 6
- stiffness: float32 [192, 4, 32, 25600], P('dom', 'grp'), may hold values from -0.5 to 0.5
- elem_faces: int32 [192, 4, 32, 4], P('dom', 'grp'), may hold values from 0 to 79, as said below
- orient: int32 [192, 4, 32, 4], P('dom', 'grp'), may hold values from 0 to 5
- counts: int32 [192, 4], P('dom', 'grp'), may hold values from 4 to 8, as said below
Outputs:
- condensed: float32 [192, 4, 80, 1280], P('dom', 'grp')
- coarse: float32 [192, 288, 384], P('dom')
Inputs may be any that keep to these rules, and one draw needn't show every extreme that they name: counts[d, g] of the 8 slots shared by partitions (d, g) and (d + 1, g) are used, slots 0 to counts[d, g] - 1; some partition uses all 8. `elem_faces`: each interior slot is named once or twice; owned slot 64 + j is named exactly once when j < counts[d, g] and never otherwise; lower slot 72 + j is named exactly once when j < counts[d - 1, g] and never otherwise (on d = 0, with the counts of the last partition along dom, naming faces on the outer boundary).
All inputs are finite; a program needn't handle non-finite values.
Results may differ from a plain program's by a relative error of at most 0.0003.
Values sent between devices are 32-bit elements; how exact they have to be, the bound alone decides.
A program may use at most 32 MiB of HBM per device.

v0:
```python
import jax
import jax.numpy as jnp
import numpy as np
from jax import lax
from jax.sharding import PartitionSpec as P

NODES = 10
INNER = 64
TRACE = 160


def from_behind(array, axis, by):
    devices = lax.axis_size(axis)
    pairs = [(i, i + by) for i in range(devices) if 0 <= i + by < devices]
    return lax.ppermute(array, axis, pairs)


def face_tables():
    node_list = [(a, b, 3 - a - b) for a in range(4) for b in range(4 - a)]
    orderings = [(0, 1, 2), (1, 2, 0), (2, 0, 1), (0, 2, 1), (2, 1, 0), (1, 0, 2)]
    node_table = np.zeros((6, 10, 10), np.float32)
    for orient_id, ordering in enumerate(orderings):
        for node_id, coords in enumerate(node_list):
            target = node_list.index(
                (coords[ordering[0]], coords[ordering[1]], coords[ordering[2]])
            )
            node_table[orient_id, node_id, target] = 1.0
    barycentric = np.array(node_list, np.float32) / 3.0
    return (node_table, barycentric)


def apply_elements(local_trace, stiffness, elem_faces, orient):
    node_table, barycentric = face_tables()
    elements = stiffness.shape[0]
    row_width = local_trace.shape[1] // NODES
    matrices = stiffness.reshape(elements, TRACE, TRACE)
    picked = local_trace[elem_faces].reshape(elements, 4, NODES, row_width)
    onehot = (orient[..., None] == jnp.arange(6, dtype=jnp.int32)).astype(local_trace.dtype)
    selector = jnp.einsum(
        "efo,onm->efnm",
        onehot,
        jnp.asarray(node_table, local_trace.dtype),
        precision=lax.Precision.HIGHEST,
    )
    values = jnp.einsum("efnm,efmc->efnc", selector, picked, precision=lax.Precision.HIGHEST)
    values = values.reshape(elements, TRACE, -1)
    result = jnp.einsum("eij,ejr->eir", matrices, values, precision=lax.Precision.HIGHEST)
    result = result.reshape(elements, 4, NODES, row_width)
    returned = jnp.einsum("efnm,efnc->efmc", selector, result, precision=lax.Precision.HIGHEST)
    returned = returned.reshape(elements * 4, NODES * row_width)
    return jax.ops.segment_sum(returned, elem_faces.reshape(-1), num_segments=local_trace.shape[0])


def body(trace, rhs, stiffness, elem_faces, orient, counts):
    node_table, barycentric = face_tables()
    owned = trace[0, 0]
    inner_count = INNER
    owned_count = owned.shape[0]
    from_below = from_behind(owned[inner_count:], "dom", 1)
    local_trace = jnp.concatenate([owned, from_below], axis=0)
    partial_value = apply_elements(local_trace, stiffness[0, 0], elem_faces[0, 0], orient[0, 0])
    interior = partial_value[:inner_count]
    part_owned = partial_value[inner_count:owned_count]
    part_lower = partial_value[owned_count:]
    from_above = from_behind(part_lower, "dom", -1)
    owned_full = part_owned + from_above
    returned_sums = from_behind(owned_full, "dom", 1)
    is_first = lax.axis_index("dom") == 0
    lower_full = jnp.where(is_first, part_lower, returned_sums)
    condensed = jnp.concatenate([interior, owned_full, lower_full], axis=0)
    residual = rhs[0, 0] - condensed[:owned_count]
    row_index = jnp.arange(owned_count, dtype=jnp.int32)
    keep_rows = row_index < inner_count + counts[0, 0]
    residual = jnp.where(keep_rows[:, None], residual, jnp.zeros_like(residual))
    residual = residual.reshape(owned_count, NODES, -1)
    coarse = jnp.einsum(
        "nv,fnc->fvc",
        jnp.asarray(barycentric, residual.dtype),
        residual,
        precision=lax.Precision.HIGHEST,
    )
    coarse = coarse.reshape(owned_count, -1)
    gathered = lax.all_gather(coarse, "grp", axis=0, tiled=True)
    return (condensed[None, None], gathered[None])


def solution(mesh):
    in_specs = (
        P("dom", "grp", None, None),
        P("dom", "grp", None, None),
        P("dom", "grp", None, None),
        P("dom", "grp", None, None),
        P("dom", "grp", None, None),
        P("dom", "grp"),
    )
    out_specs = (P("dom", "grp", None, None), P("dom", None, None))
    return jax.shard_map(body, mesh=mesh, in_specs=in_specs, out_specs=out_specs, check_vma=False)
```

profile of v0, /device:TPU:56, one launch (start us, length us, event | category | flops | bytes accessed | tf_op | source)
XLA Modules:
  0.0 70.7 jit_solution(15299649919465667249)
XLA Ops:
  0.6 0.8 %slice_bitcast_fusion = f32[8,1280]{1,0:T(8,128)S(1)} fusion(f32[1,1,72,1280]{3,2,1,0:T(8,128)} %param.8), kind=kLoop, calls=%fused_computation.18 | loop fusion | bytes 81920 | tf_op jit(solution)/shard_map/slice | solution.py:59
  1.4 1.9 %collective-permute-start = (f32[8,1280]{1,0:T(8,128)S(1)}, f32[8,1280]{1,0:T(8,128)S(1)}, u32[]{:S(2)}, u32[]{:S(2)}) collective-permute-start(f32[8,1280]{1,0:T(8,128)S(1)} %slice_bitcast_fusion), channel_id=1, source_target_pairs={{0,4},{4,8},{8,12},{12,16},{16,20},{20,24},{24,28},{28,32},{32,36}... | collective-permute-start | bytes 122888 | tf_op jit(solution)/shard_map/ppermute | solution.py:15
  3.3 0.7 compare_select_fusion
  4.2 1.1 %fusion.12 = f32[32,4,10,10]{0,3,2,1:T(8,128)S(1)} fusion(f32[6,10,10,1]{2,0,1,3:T(8,128)} %constant.28, s32[32,4]{0,1:T(4,128)} %bitcast.52), kind=kOutput, calls=%fused_computation.22 | convolution fusion | flops 922368 | bytes 54112 | tf_op jit(solution)/shard_map/efo,onm->efnm/dot_general | solution.py:39
  5.4 0.8 %copy.22 = s32[1,1,32,4]{3,2,1,0:T(8,128)S(1)} copy(s32[1,1,32,4]{2,3,1,0:T(4,128)} %param.11) | data formatting | bytes 1024 | tf_op args[3]
  6.1 1.0 %copy.27 = f32[32,4,10,10]{2,3,1,0:T(8,128)S(1)} copy(f32[32,4,10,10]{0,3,2,1:T(8,128)S(1)} %fusion.12) | data formatting | bytes 102400 | tf_op jit(solution)/shard_map/efo,onm->efnm/dot_general | solution.py:39
  7.2 6.4 %reshape_squeeze.3 = f32[32,160,160]{2,1,0:T(8,128)} reshape(f32[1,1,32,25600]{3,2,1,0:T(8,128)} %param.10) | data formatting | bytes 6553600 | tf_op jit(solution)/shard_map/reshape;squeeze | solution.py:36
  14.4 3.5 %collective-permute-done = f32[8,1280]{1,0:T(8,128)S(1)} collective-permute-done((f32[8,1280]{1,0:T(8,128)S(1)}, f32[8,1280]{1,0:T(8,128)S(1)}, u32[]{:S(2)}, u32[]{:S(2)}) %collective-permute-start) | collective-permute-done | bytes 40992 | tf_op jit(solution)/shard_map/ppermute | solution.py:15
  17.9 0.9 %gather_fusion = f32[128,1280]{1,0:T(8,128)S(1)} fusion(f32[80,1280]{1,0:T(8,128)S(1)} %pad_maximum_fusion, s32[1024]{0:T(1024)S(1)} %pad_clamp_fusion), kind=kCustom, calls=%fused_computation | custom fusion | bytes 1311232 | tf_op jit(solution)/shard_map/gather | solution.py:37
  18.8 0.1 reshape.63
  18.9 2.8 %fusion.17 = f32[32,4,10,128]{3,2,1,0:T(8,128)} fusion(f32[32,4,10,10]{2,3,1,0:T(8,128)S(1)} %copy.27, f32[32,4,10,128]{3,2,1,0:T(8,128)S(1)} %reshape.63), kind=kOutput, calls=%fused_computation.29 | convolution fusion | flops 19660800 | bytes 1361920 | tf_op jit(solution)/shard_map/efnm,efmc->efnc/dot_general | solution.py:45
  21.7 1.7 %reshape.64 = f32[32,160,32]{2,1,0:T(8,128)S(1)} reshape(f32[32,4,10,128]{3,2,1,0:T(8,128)} %fusion.17) | data formatting | bytes 1310720 | tf_op jit(solution)/shard_map/reshape | solution.py:46
  23.5 8.9 %convolution_bitcast_fusion = f32[32,160,32]{1,2,0:T(8,128)} fusion(f32[32,160,32]{2,1,0:T(8,128)S(1)} %reshape.64, f32[32,160,160]{2,1,0:T(8,128)} %reshape_squeeze.3), kind=kOutput, calls=%fused_computation.2 | convolution fusion | flops 314572800 | bytes 4587520 | tf_op jit(solution)/shard_map/eij,ejr->eir/dot_general | solution.py:47
  32.4 1.9 %copy.26 = f32[32,160,32]{2,1,0:T(8,128)S(1)} copy(f32[32,160,32]{1,2,0:T(8,128)} %convolution_bitcast_fusion) | data formatting | bytes 1310720 | tf_op jit(solution)/shard_map/eij,ejr->eir/dot_general | solution.py:47
  34.3 1.6 %reshape.65 = f32[32,4,10,128]{3,2,1,0:T(8,128)} reshape(f32[32,160,32]{2,1,0:T(8,128)S(1)} %copy.26) | data formatting | bytes 1310720 | tf_op jit(solution)/shard_map/reshape | solution.py:48
  35.9 2.7 %fusion.18 = f32[32,4,10,128]{3,2,1,0:T(8,128)S(1)} fusion(f32[32,4,10,10]{2,3,1,0:T(8,128)} %copy-done, f32[32,4,10,128]{3,2,1,0:T(8,128)} %reshape.65), kind=kOutput, calls=%fused_computation.30 | convolution fusion | flops 19660800 | bytes 1361920 | tf_op jit(solution)/shard_map/efnm,efnc->efmc/dot_general | solution.py:49
  38.6 2.0 %scatter_custom_fusion = f32[80,1280]{1,0:T(8,128)S(1)} fusion(s32[128]{0:T(128)S(1)} %reshape.78, f32[16,8,10,128]{3,2,1,0:T(8,128)S(1)} %bitcast.46, f32[]{:T(128)} %constant.8.clone.1), kind=kCustom, calls=%fused_computation.3 | custom fusion | flops 163840 | bytes 1458180 | tf_op jit(solution)/shard_map/scatter-add | solution.py:51
  40.6 11.3 %collective-permute-start.1 = (f32[8,1280]{1,0:T(8,128)S(1)}, f32[8,1280]{1,0:T(8,128)S(1)}, u32[]{:S(2)}, u32[]{:S(2)}) collective-permute-start(f32[8,1280]{1,0:T(8,128)S(1)} %slice.26), channel_id=1, source_target_pairs={{4,0},{8,4},{12,8},{16,12},{20,16},{24,20},{28,24},{32,28},{36,32}... | collective-permute-start | bytes 122888 | tf_op jit(solution)/shard_map/ppermute | solution.py:15
  52.1 1.4 %collective-permute-done.1 = f32[8,1280]{1,0:T(8,128)S(1)} collective-permute-done((f32[8,1280]{1,0:T(8,128)S(1)}, f32[8,1280]{1,0:T(8,128)S(1)}, u32[]{:S(2)}, u32[]{:S(2)}) %collective-permute-start.1) | collective-permute-done | bytes 40992 | tf_op jit(solution)/shard_map/ppermute | solution.py:15
  53.6 1.9 %collective-permute-start.2 = (f32[8,1280]{1,0:T(8,128)S(1)}, f32[8,1280]{1,0:T(8,128)S(1)}, u32[]{:S(2)}, u32[]{:S(2)}) collective-permute-start(f32[8,1280]{1,0:T(8,128)S(1)} %slice_add_fusion), channel_id=1, source_target_pairs={{0,4},{4,8},{8,12},{12,16},{16,20},{20,24},{24,28},{28,32},{32,36}... | collective-permute-start | bytes 122888 | tf_op jit(solution)/shard_map/ppermute | solution.py:15
  55.5 0.6 fusion.4
  56.1 13.0 %all_gather.3 = f32[288,384]{1,0:T(8,128)S(1)} all-gather(f32[72,384]{1,0:T(8,128)S(1)} %bitcast.50), channel_id=1, replica_groups=mesh['dom'=192,'grp'=4] {'grp'}, dimensions={0}, use_global_device_ids=true | all-gather | bytes 552960 | tf_op jit(solution)/shard_map/all_gather | solution.py:83
  69.1 0.8 %maximum_bitcast_fusion = f32[1,1,80,1280]{3,2,1,0:T(8,128)} fusion(f32[8,1280]{1,0:T(8,128)S(1)} %broadcast_select_fusion, f32[8,1280]{1,0:T(8,128)S(1)} %slice_add_fusion, f32[64,1280]{1,0:T(8,128)S(1)} %slice.24), kind=kLoop, calls=%fused_computation.12 | loop fusion | flops 204800 | bytes 819200 | tf_op jit(solution)/shard_map/broadcast_in_dim | solution.py:84
  69.9 0.8 %copy.41 = f32[1,288,384]{2,1,0:T(8,128)} copy(f32[1,288,384]{2,1,0:T(8,128)S(1)} %bitcast.47) | data formatting | bytes 884736
  (23 shorter events, 0.5 us)
Async XLA Ops:
  1.4 16.5 %collective-permute-start = (f32[8,1280]{1,0:T(8,128)S(1)}, f32[8,1280]{1,0:T(8,128)S(1)}, u32[]{:S(2)}, u32[]{:S(2)}) collective-permute-start(f32[8,1280]{1,0:T(8,128)S(1)} %slice_bitcast_fusion), channel_id=1, source_target_pairs={{0,4},{4,8},{8,12},{12,16},{16,20},{20,24},{24,28},{28,32},{32,36}... | collective-permute-start | bytes 122888 | tf_op jit(solution)/shard_map/ppermute | solution.py:15
  7.1 11.8 %copy-start = (f32[32,4,10,10]{2,3,1,0:T(8,128)}, f32[32,4,10,10]{2,3,1,0:T(8,128)S(1)}, u32[]{:S(2)}) copy-start(f32[32,4,10,10]{2,3,1,0:T(8,128)S(1)} %copy.27) | copy-start | bytes 153604
  7.2 10.7 %copy-start.1 = (f32[1,1,72,1280]{3,2,1,0:T(8,128)S(1)}, f32[1,1,72,1280]{3,2,1,0:T(8,128)}, u32[]{:S(2)}) copy-start(f32[1,1,72,1280]{3,2,1,0:T(8,128)} %param.8) | copy-start | bytes 1105924
  34.3 17.7 %copy-start.2 = (f32[1,1,72,1280]{3,2,1,0:T(8,128)S(1)}, f32[1,1,72,1280]{3,2,1,0:T(8,128)}, u32[]{:S(2)}) copy-start(f32[1,1,72,1280]{3,2,1,0:T(8,128)} %param.9) | copy-start | bytes 1105924
  35.9 19.7 %copy-start.3 = (f32[10,3,1]{0,1,2:T(4,128)S(1)}, f32[10,3,1]{0,1,2:T(4,128)}, u32[]{:S(2)}) copy-start(f32[10,3,1]{0,1,2:T(4,128)} %constant.29) | copy-start | bytes 364
  40.6 13.0 %collective-permute-start.1 = (f32[8,1280]{1,0:T(8,128)S(1)}, f32[8,1280]{1,0:T(8,128)S(1)}, u32[]{:S(2)}, u32[]{:S(2)}) collective-permute-start(f32[8,1280]{1,0:T(8,128)S(1)} %slice.26), channel_id=1, source_target_pairs={{4,0},{8,4},{12,8},{16,12},{20,16},{24,20},{28,24},{32,28},{36,32}... | collective-permute-start | bytes 122888 | tf_op jit(solution)/shard_map/ppermute | solution.py:15
  53.6 15.5 %collective-permute-start.2 = (f32[8,1280]{1,0:T(8,128)S(1)}, f32[8,1280]{1,0:T(8,128)S(1)}, u32[]{:S(2)}, u32[]{:S(2)}) collective-permute-start(f32[8,1280]{1,0:T(8,128)S(1)} %slice_add_fusion), channel_id=1, source_target_pairs={{0,4},{4,8},{8,12},{12,16},{16,20},{20,24},{24,28},{28,32},{32,36}... | collective-permute-start | bytes 122888 | tf_op jit(solution)/shard_map/ppermute | solution.py:15
where the time goes:
time: 71.2 us; the launch traced here: 70.7 us
  local copies, waits for them, and re-layouts  16.4 us (23%)
  matrix products  16.1 us (23%)
  starting transfers between devices  15.1 us (21%)
  blocking collectives  13 us (18%)
  waiting for transfers between devices  4.98 us (7%)
  other arithmetic  3.56 us (5%)
  between operations  1.52 us (2%)
    ppermute x3, starting transfers between devices, from_behind(): return lax.ppermute(array, axis, pairs)  15.1 us
    all_gather x1, blocking collectives, body(): gathered = lax.all_gather(coarse, 'grp', axis=0, tiled=True)  13 us
    dot_general x1, matrix products, apply_elements(): jnp.einsum('eij,ejr->eir', matrices, values, precision=lax.Precision.HIGH...  8.88 us
    another operation x1, local copies, waits for them, and re-layouts, apply_elements(): matrices = stiffness.reshape(elements, TRACE, TRACE)  6.44 us
    ppermute x3, waiting for transfers between devices, from_behind(): return lax.ppermute(array, axis, pairs)  4.98 us
    dot_general x1, matrix products, apply_elements(): jnp.einsum('efnm,efmc->efnc', selector, picked, precision=lax.Precision.H...  2.81 us
    dot_general x1, matrix products, apply_elements(): jnp.einsum('efnm,efnc->efmc', selector, result, precision=lax.Precision.H...  2.7 us
    scatter-add x1, other arithmetic, apply_elements(): jax.ops.segment_sum(returned, elem_faces.reshape(-1), num_segments=local_...  2.03 us
  transfers between devices with their start and end apart: 3, of which 2 were waited for; matrix products, arithmetic and copies ran while one was open for 16% of the time, Pallas kernels for 0%

commit v1 on v0

v1 whole, which is shorter than its diff:
```python
import jax
import jax.numpy as jnp
import numpy as np
from jax import lax
from jax.experimental import pallas as pl
from jax.experimental.pallas import tpu as pltpu
from jax.sharding import PartitionSpec as P

F32 = jnp.float32
BF16 = jnp.bfloat16
MESH = pl.DeviceIdType.MESH
ELEMS = 32
NODES = 10
INNER = 64
OWN = 72
SLOTS = 80
ROW = 1280
COARSE = 384
HEAD = 40

NODE_LIST = [(a, b, 3 - a - b) for a in range(4) for b in range(4 - a)]
ORDERINGS = [(0, 1, 2), (1, 2, 0), (2, 0, 1), (0, 2, 1), (2, 1, 0), (1, 0, 2)]
PERM = [
    [NODE_LIST.index((c[p[0]], c[p[1]], c[p[2]])) for c in NODE_LIST] for p in ORDERINGS
]
INVERSE = [[row.index(m) for m in range(NODES)] for row in PERM]
BARY = np.array(NODE_LIST, np.float32) / np.float32(3.0)


def split(x):
    high = x.astype(BF16)
    return high, (x - high.astype(F32)).astype(BF16)


def dot(a, b):
    return jnp.dot(a, b, preferred_element_type=F32)


def iota(shape, dim):
    return lax.broadcasted_iota(jnp.int32, shape, dim)


def spread(small):
    pick = (iota((128, 4), 0) % 4 == iota((128, 4), 1)).astype(F32).astype(BF16)
    rows = dot(pick, small.astype(F32).astype(BF16))
    rows = jnp.where(iota((128, ELEMS), 0) // 4 == iota((128, ELEMS), 1), rows, 0.0)
    return dot(rows.astype(BF16), jnp.ones((ELEMS, 128), BF16))


def oriented(orient, slabs, table, node):
    if all(table[o][node] == node for o in range(6)):
        return slabs[node]
    out = slabs[table[5][node]]
    for o in range(4, -1, -1):
        out = jnp.where(orient == o, slabs[table[o][node]], out)
    return out


def build_selectors(faces_ref, orient_ref, pick_ref, back_ref, turn_ref):
    faces = spread(faces_ref[...])
    turn_ref[...] = spread(orient_ref[...])
    pick = (faces == iota((128, 128), 1).astype(F32)).astype(F32)
    pick_ref[:, :128] = pick.astype(BF16)
    pick_ref[:, 128:] = pick.astype(BF16)
    back = pick.T.astype(BF16)
    back_ref[:, :128] = back
    back_ref[:, 128:] = back


def gather_values(local_ref, pick_ref, turn_ref, pieces_ref, values_ref):
    high, low = split(local_ref[...])
    nothing = jnp.zeros((128 - SLOTS, ROW), BF16)
    pieces_ref[0:80, :] = high
    pieces_ref[80:128, :] = nothing
    pieces_ref[128:208, :] = low
    pieces_ref[208:256, :] = nothing
    pick = pick_ref[...]
    slabs = []
    for pair in range(NODES // 2):
        both = dot(pick, pieces_ref[:, pair * 256 : (pair + 1) * 256])
        slabs += [both[:, :128], both[:, 128:]]
    turn = turn_ref[...]
    group = iota((128, 128), 1) // 32
    for node in range(NODES):
        value = oriented(turn, slabs, PERM, node)
        moved = [value] + [pltpu.roll(value, 32 * s, 1) for s in (1, 2, 3)]
        for field in range(4):
            out = moved[(3 - field) % 4]
            for g in (2, 1, 0):
                out = jnp.where(group == g, moved[(g - field) % 4], out)
            values_ref[pl.ds(node * 4 + field, 128, stride=40), :] = out


def element_product(e, matrix_ref, values_ref, result_ref):
    values = values_ref[pl.ds(e * 160, 160), :]
    lane = iota((40, 128), 1)
    group = lane // 32
    high, low = split(values[:128])
    main = jnp.concatenate([high, low], axis=1)
    main = jnp.concatenate([main, main], axis=0)
    last = values[128:160]
    group32 = iota((32, 128), 1) // 32
    rest = jnp.concatenate([jnp.where(group32 == b, last, 0.0) for b in range(4)], axis=0)
    high, low = split(rest)
    rest = jnp.concatenate([high, low], axis=1)
    rest = jnp.concatenate([rest, rest], axis=0)
    parts = [matrix_ref[e, pl.ds(c, 40, stride=5), :] for c in range(5)]
    rows = [parts[0]]
    for b in range(1, 4):
        mixed = jnp.where(lane >= 32 * b, parts[b], parts[b + 1])
        rows.append(pltpu.roll(mixed, 128 - 32 * b, 1))
    high, low = split(jnp.concatenate(rows, axis=0))
    first = dot(jnp.concatenate([high, low], axis=1), main)
    tail = jnp.where(
        group == 0, parts[1], jnp.where(group == 1, parts[2], jnp.where(group == 2, parts[3], parts[4]))
    )
    high, low = split(tail)
    second = dot(jnp.concatenate([high, low], axis=1), rest)
    first = first[:, :128] + first[:, 128:]
    second = second[:, :128] + second[:, 128:]
    out = jnp.where(
        group == 0,
        first[0:40],
        jnp.where(group == 1, first[40:80], jnp.where(group == 2, first[80:120], first[120:160])),
    )
    result_ref[pl.ds(e * 40, 40), :] = out + second


def scatter_results(result_ref, back_ref, turn_ref, partial_ref):
    turn = turn_ref[...]
    slabs = [result_ref[pl.ds(n, 128, stride=NODES), :] for n in range(NODES)]
    back = back_ref[0:SLOTS, :]
    for pair in range(NODES // 2):
        both = [oriented(turn, slabs, INVERSE, m) for m in (2 * pair, 2 * pair + 1)]
        high, low = split(jnp.concatenate(both, axis=1))
        partial_ref[:, pair * 256 : (pair + 1) * 256] = dot(back, jnp.concatenate([high, low], axis=0))


def project(rows):
    out = []
    for v in range(3):
        terms = [float(BARY[n, v]) * rows(n) for n in range(NODES) if BARY[n, v] != 0]
        total = terms[0]
        for term in terms[1:]:
            total = total + term
        out.append(total)
    return out


def kernel(
    n_dom,
    trace_hbm,
    rhs_hbm,
    matrix_hbm,
    faces_hbm,
    orient_hbm,
    counts_hbm,
    cond_ref,
    coarse_ref,
    local,
    rhs,
    matrix,
    faces,
    orient,
    counts,
    pick,
    back,
    turn,
    pieces,
    values,
    result,
    shared,
    arrived,
    low_out,
    low_in,
    in_sem,
    matrix_sem,
    dom_send,
    dom_recv,
    low_send,
    low_recv,
    grp_send,
    grp_recv,
):
    d = lax.axis_index("dom")
    g = lax.axis_index("grp")
    has_below = d > 0
    has_above = d < n_dom - 1
    right = lax.rem(g + 1, 4)
    left = lax.rem(g + 3, 4)
    opposite = lax.rem(g + 2, 4)

    loads = [
        pltpu.make_async_copy(trace_hbm, local.at[pl.ds(0, OWN)], in_sem.at[0]),
        pltpu.make_async_copy(faces_hbm, faces, in_sem.at[1]),
        pltpu.make_async_copy(orient_hbm, orient, in_sem.at[2]),
        pltpu.make_async_copy(counts_hbm, counts, in_sem.at[3]),
        pltpu.make_async_copy(rhs_hbm, rhs, in_sem.at[4]),
    ]
    for load in loads[:4]:
        load.start()

    barrier = pltpu.get_barrier_semaphore()

    def greet(dom, grp):
        pl.semaphore_signal(barrier, inc=1, device_id=(dom, grp), device_id_type=MESH)

    greet(d, right)
    greet(d, left)

    @pl.when(has_below)
    def _():
        greet(d - 1, g)

    @pl.when(has_above)
    def _():
        for i in range(4):
            greet(d + 1, lax.rem(g + i, 4))

    matrix_loads = [
        pltpu.make_async_copy(matrix_hbm.at[e // 8, :, e % 8, :], matrix.at[e], matrix_sem.at[e])
        for e in range(ELEMS)
    ]
    for load in matrix_loads:
        load.start()
    loads[4].start()

    pl.semaphore_wait(barrier, 2 + 4 * has_below.astype(jnp.int32) + has_above.astype(jnp.int32))

    def remote(src, dst, send, recv, dom, grp):
        return pltpu.make_async_remote_copy(
            src_ref=src,
            dst_ref=dst,
            send_sem=send,
            recv_sem=recv,
            device_id=(dom, grp),
            device_id_type=MESH,
        )

    trace_up = remote(
        trace_hbm.at[pl.ds(INNER, 8)], local.at[pl.ds(OWN, 8)], dom_send.at[0], dom_recv.at[0], d + 1, g
    )
    part_up = remote(shared.at[0], arrived.at[0], dom_send.at[1], dom_recv.at[1], d + 1, g)
    part_down = remote(shared.at[1], arrived.at[1], dom_send.at[2], dom_recv.at[2], d - 1, g)
    low_down = [
        remote(low_out, low_in.at[i], low_send.at[i], low_recv.at[i], d - 1, lax.rem(g + i, 4))
        for i in range(4)
    ]

    @pl.when(has_above)
    def _():
        trace_up.start()

    @pl.when(jnp.logical_not(has_below))
    def _():
        local[OWN:SLOTS, :] = jnp.zeros((8, ROW), F32)

    loads[1].wait()
    loads[2].wait()
    build_selectors(faces, orient, pick, back, turn)
    loads[0].wait()

    @pl.when(has_below)
    def _():
        trace_up.wait_recv()

    gather_values(local, pick, turn, pieces, values)
    for load in matrix_loads:
        load.wait()

    def step(e, carry):
        element_product(e, matrix, values, result)
        return carry

    lax.fori_loop(0, ELEMS, step, 0, unroll=8)
    scatter_results(result, back, turn, cond_ref)

    shared[0] = cond_ref[INNER:OWN, :]
    shared[1] = cond_ref[OWN:SLOTS, :]
    low = project(lambda n: cond_ref[OWN:SLOTS, n * 128 : (n + 1) * 128])
    for v in range(3):
        low_out[:, v * 128 : (v + 1) * 128] = low[v]

    @pl.when(has_below)
    def _():
        part_down.start()
        for copy in low_down:
            copy.start()

    @pl.when(has_above)
    def _():
        part_up.start()

    loads[3].wait()
    loads[4].wait()
    mine = pl.multiple_of(g * OWN, 8)
    own = project(
        lambda n: rhs[:, n * 128 : (n + 1) * 128] - cond_ref[0:OWN, n * 128 : (n + 1) * 128]
    )
    keep = iota((OWN, 128), 0) < INNER + counts[...]
    for v in range(3):
        coarse_ref[pl.ds(mine, OWN), v * 128 : (v + 1) * 128] = jnp.where(keep, own[v], 0.0)

    def piece(owner, which):
        start = pl.multiple_of(owner * OWN + HEAD * which, 8)
        return coarse_ref.at[pl.ds(start, (HEAD, OWN - HEAD)[which])]

    def pass_on(owner, which, number, to):
        return remote(
            piece(owner, which),
            piece(owner, which),
            grp_send.at[number],
            grp_recv.at[number],
            d,
            to,
        )

    sends = [
        pass_on(g, 0, 0, right),
        pass_on(g, 1, 1, left),
        pass_on(g, 1, 2, right),
        pass_on(g, 0, 3, left),
    ]
    for copy in sends:
        copy.start()
    onward = [pass_on(left, 0, 4, right), pass_on(right, 1, 5, left)]

    def arrival(owner, which, number):
        return remote(
            piece(owner, which),
            piece(owner, which),
            grp_send.at[number],
            grp_recv.at[number],
            d,
            right,
        )

    arrival(left, 0, 0).wait_recv()
    onward[0].start()
    arrival(right, 1, 1).wait_recv()
    onward[1].start()

    @pl.when(has_above)
    def _():
        part_down.wait_recv()
        cond_ref[INNER:OWN, :] = shared[0] + arrived[1]

    @pl.when(has_below)
    def _():
        part_up.wait_recv()
        cond_ref[OWN:SLOTS, :] = shared[1] + arrived[0]

    arrival(left, 1, 2).wait_recv()
    arrival(right, 0, 3).wait_recv()
    for copy in sends:
        copy.wait_send()
    for copy in onward:
        copy.wait_send()
    arrival(opposite, 0, 4).wait_recv()
    arrival(opposite, 1, 5).wait_recv()

    @pl.when(has_above)
    def _():
        for i in range(4):
            low_down[i].wait_recv()
            owner = lax.rem(g + 4 - i, 4)
            rows = pl.ds(pl.multiple_of(owner * OWN + INNER, 8), 8)
            coarse_ref[rows, :] = coarse_ref[rows, :] - low_in[i]

    @pl.when(has_above)
    def _():
        trace_up.wait_send()
        part_up.wait_send()

    @pl.when(has_below)
    def _():
        part_down.wait_send()
        for copy in low_down:
            copy.wait_send()


def body(trace, rhs, stiffness, elem_faces, orient, counts):
    n_dom = lax.axis_size("dom")
    matrix = stiffness.reshape(4, 8, 200, 128).transpose(0, 2, 1, 3)
    hbm = pl.BlockSpec(memory_space=pl.ANY)
    vmem = pl.BlockSpec(memory_space=pltpu.VMEM)
    dma = pltpu.SemaphoreType.DMA
    cond, coarse = pl.pallas_call(
        lambda *refs: kernel(n_dom, *refs),
        out_shape=(
            jax.ShapeDtypeStruct((SLOTS, ROW), F32),
            jax.ShapeDtypeStruct((4 * OWN, COARSE), F32),
        ),
        in_specs=[hbm] * 6,
        out_specs=(vmem, vmem),
        scratch_shapes=[
            pltpu.VMEM((SLOTS, ROW), F32),
            pltpu.VMEM((OWN, ROW), F32),
            pltpu.VMEM((ELEMS, 200, 128), F32),
            pltpu.VMEM((4, ELEMS), jnp.int32),
            pltpu.VMEM((4, ELEMS), jnp.int32),
            pltpu.VMEM((1, 1), jnp.int32),
            pltpu.VMEM((128, 256), BF16),
            pltpu.VMEM((128, 256), BF16),
            pltpu.VMEM((128, 128), F32),
            pltpu.VMEM((256, ROW), BF16),
            pltpu.VMEM((ELEMS * 160, 128), F32),
            pltpu.VMEM((ELEMS * 40, 128), F32),
            pltpu.VMEM((2, 8, ROW), F32),
            pltpu.VMEM((2, 8, ROW), F32),
            pltpu.VMEM((8, COARSE), F32),
            pltpu.VMEM((4, 8, COARSE), F32),
            dma((5,)),
            dma((ELEMS,)),
            dma((3,)),
            dma((3,)),
            dma((4,)),
            dma((4,)),
            dma((6,)),
            dma((6,)),
        ],
        compiler_params=pltpu.CompilerParams(
            collective_id=0, has_side_effects=True, vmem_limit_bytes=60 * 2**20
        ),
    )(
        trace[0, 0],
        rhs[0, 0],
        matrix,
        elem_faces[0, 0].T,
        orient[0, 0].T,
        counts,
    )
    return cond[None, None], coarse[None]


def solution(mesh):
    part = P("dom", "grp", None, None)
    return jax.shard_map(
        body,
        mesh=mesh,
        in_specs=(part, part, part, part, part, P("dom", "grp")),
        out_specs=(part, P("dom", None, None)),
        check_vma=False,
    )
```

time: 71.2 us -> 35.6 us (0.50)
  Pallas kernels: 0 us -> 30.5 us
  matrix products: 16.1 us -> 0 us
  starting transfers between devices: 15.1 us -> 0 us
  blocking collectives: 13 us -> 0 us
  local copies, waits for them, and re-layouts: 16.4 us -> 3.58 us
  waiting for transfers between devices: 4.98 us -> 0 us
  other arithmetic: 3.56 us -> 0 us
    pallas_call x0 -> x1, Pallas kernels: none -> 30.5 us  [body(): pl.pallas_call(lambda *refs: kernel(n_dom, *refs), out_shape=(jax.ShapeDt...]
    dot_general x5 -> x0, matrix products: 16.1 us -> none  [the longest x1 8.88 us: apply_elements(): jnp.einsum('eij,ejr->eir', matrices, values, precision=lax.Precision.HIGH...]
    ppermute x3 -> x0, starting transfers between devices: 15.1 us -> none  [from_behind(): return lax.ppermute(array, axis, pairs)]
    all_gather x1 -> x0, blocking collectives: 13 us -> none  [body(): gathered = lax.all_gather(coarse, 'grp', axis=0, tiled=True)]
    another operation x2 -> x0, local copies, waits for them, and re-layouts: 6.54 us -> none  [the longest x1 6.44 us: apply_elements(): matrices = stiffness.reshape(elements, TRACE, TRACE)]
    ppermute x3 -> x0, waiting for transfers between devices: 4.98 us -> none  [from_behind(): return lax.ppermute(array, axis, pairs)]
    reshape x3 -> x0, local copies, waits for them, and re-layouts: 3.41 us -> none  [the longest x1 1.75 us: apply_elements(): values = values.reshape(elements, TRACE, -1)]
    dot_general x2 -> x0, local copies, waits for them, and re-layouts: 2.91 us -> none  [the longest x1 1.91 us: apply_elements(): jnp.einsum('eij,ejr->eir', matrices, values, precision=lax.Precision.HIGH...]
  transfers between devices with their start and end apart: 3 -> 0, of which waited for: 2 -> 0; matrix products, arithmetic and copies ran while one was open for 16% -> 0% of each run, Pallas kernels for 0% -> 0%
where the time goes in v1:
time: 35.6 us; the launch traced here: 35.4 us
  Pallas kernels  30.5 us (86%)
  local copies, waits for them, and re-layouts  3.58 us (10%)
  between operations  1.29 us (4%)
    pallas_call x1, Pallas kernels, body(): pl.pallas_call(lambda *refs: kernel(n_dom, *refs), out_shape=(jax.ShapeDt...  30.5 us
    unnamed x2, local copies, waits for them, and re-layouts  3.58 us

profile of v1, /device:TPU:56, one launch (start us, length us, event | category | flops | bytes accessed | tf_op | source)
XLA Modules:
  0.0 35.4 jit_solution(14121819274916014517)
XLA Ops:
  1.3 30.5 %shard_map.77 = (f32[80,1280]{1,0:T(8,128)}, f32[288,384]{1,0:T(8,128)}) custom-call(f32[72,1280]{1,0:T(8,128)} %bitcast.16, f32[72,1280]{1,0:T(8,128)} %bitcast.17, f32[4,200,8,128]{3,2,1,0:T(8,128)} %bitcast.13, s32[4,32]{1,0:T(4,128)} %bitcast.18, s32[4,32]{1,0:T(4,128)} %bitcast.19, s32[1,1]{1,0:T(1,128)S(6)} %copy.10.refs_5_), custom_call_target="tpu_custom_call" | custom-call | tf_op jit(solution)/shard_map/pallas_call | solution.py:388
  31.8 1.8 %copy.11 = f32[1,1,80,1280]{3,2,1,0:T(8,128)} copy(f32[1,1,80,1280]{3,2,1,0:T(8,128)} %bitcast.15) | data formatting | bytes 819200
  33.6 1.8 %copy.12 = f32[1,288,384]{2,1,0:T(8,128)} copy(f32[1,288,384]{2,1,0:T(8,128)} %bitcast.14) | data formatting | bytes 884736

commit v2 on v1

--- a/solution.py
+++ b/solution.py
@@ -154,7 +154,6 @@
     matrix_hbm,
     faces_hbm,
     orient_hbm,
-    counts_hbm,
     cond_ref,
     coarse_ref,
     local,
@@ -162,7 +161,6 @@
     matrix,
     faces,
     orient,
-    counts,
     pick,
     back,
     turn,
@@ -194,10 +192,9 @@
         pltpu.make_async_copy(trace_hbm, local.at[pl.ds(0, OWN)], in_sem.at[0]),
         pltpu.make_async_copy(faces_hbm, faces, in_sem.at[1]),
         pltpu.make_async_copy(orient_hbm, orient, in_sem.at[2]),
-        pltpu.make_async_copy(counts_hbm, counts, in_sem.at[3]),
-        pltpu.make_async_copy(rhs_hbm, rhs, in_sem.at[4]),
+        pltpu.make_async_copy(rhs_hbm, rhs, in_sem.at[3]),
     ]
-    for load in loads[:4]:
+    for load in loads[:3]:
         load.start()
 
     barrier = pltpu.get_barrier_semaphore()
@@ -223,7 +220,7 @@
     ]
     for load in matrix_loads:
         load.start()
-    loads[4].start()
+    loads[3].start()
 
     pl.semaphore_wait(barrier, 2 + 4 * has_below.astype(jnp.int32) + has_above.astype(jnp.int32))
 
@@ -265,14 +262,16 @@
         trace_up.wait_recv()
 
     gather_values(local, pick, turn, pieces, values)
-    for load in matrix_loads:
-        load.wait()
-
-    def step(e, carry):
-        element_product(e, matrix, values, result)
+
+    def block(i, carry):
+        for q in range(8):
+            e = i * 8 + q
+            pltpu.make_async_copy(matrix_hbm.at[0, :, 0, :], matrix.at[e], matrix_sem.at[e]).wait()
+        for q in range(8):
+            element_product(i * 8 + q, matrix, values, result)
         return carry
 
-    lax.fori_loop(0, ELEMS, step, 0, unroll=8)
+    lax.fori_loop(0, ELEMS // 8, block, 0)
     scatter_results(result, back, turn, cond_ref)
 
     shared[0] = cond_ref[INNER:OWN, :]
@@ -292,12 +291,12 @@
         part_up.start()
 
     loads[3].wait()
-    loads[4].wait()
     mine = pl.multiple_of(g * OWN, 8)
     own = project(
         lambda n: rhs[:, n * 128 : (n + 1) * 128] - cond_ref[0:OWN, n * 128 : (n + 1) * 128]
     )
-    keep = iota((OWN, 128), 0) < INNER + counts[...]
+    named = dot(back[0:SLOTS, :128], jnp.ones((128, 128), BF16))[:OWN]
+    keep = jnp.logical_or(iota((OWN, 128), 0) < INNER, named > 0.5)
     for v in range(3):
         coarse_ref[pl.ds(mine, OWN), v * 128 : (v + 1) * 128] = jnp.where(keep, own[v], 0.0)
 
@@ -379,6 +378,19 @@
             copy.wait_send()
 
 
+def write_out(cond, coarse, cond_out, coarse_out, sem):
+    copies = []
+    for half in range(2):
+        rows = pl.ds(half * 40, 40)
+        copies.append(pltpu.make_async_copy(cond.at[rows], cond_out.at[rows], sem.at[half]))
+        rows = pl.ds(half * 144, 144)
+        copies.append(pltpu.make_async_copy(coarse.at[rows], coarse_out.at[rows], sem.at[2 + half]))
+    for copy in copies:
+        copy.start()
+    for copy in copies:
+        copy.wait()
+
+
 def body(trace, rhs, stiffness, elem_faces, orient, counts):
     n_dom = lax.axis_size("dom")
     matrix = stiffness.reshape(4, 8, 200, 128).transpose(0, 2, 1, 3)
@@ -388,10 +400,10 @@
     cond, coarse = pl.pallas_call(
         lambda *refs: kernel(n_dom, *refs),
         out_shape=(
-            jax.ShapeDtypeStruct((SLOTS, ROW), F32),
-            jax.ShapeDtypeStruct((4 * OWN, COARSE), F32),
+            pltpu.VMEM((SLOTS, ROW), F32),
+            pltpu.VMEM((4 * OWN, COARSE), F32),
         ),
-        in_specs=[hbm] * 6,
+        in_specs=[hbm] * 5,
         out_specs=(vmem, vmem),
         scratch_shapes=[
             pltpu.VMEM((SLOTS, ROW), F32),
@@ -399,7 +411,6 @@
             pltpu.VMEM((ELEMS, 200, 128), F32),
             pltpu.VMEM((4, ELEMS), jnp.int32),
             pltpu.VMEM((4, ELEMS), jnp.int32),
-            pltpu.VMEM((1, 1), jnp.int32),
             pltpu.VMEM((128, 256), BF16),
             pltpu.VMEM((128, 256), BF16),
             pltpu.VMEM((128, 128), F32),
@@ -410,7 +421,7 @@
             pltpu.VMEM((2, 8, ROW), F32),
             pltpu.VMEM((8, COARSE), F32),
             pltpu.VMEM((4, 8, COARSE), F32),
-            dma((5,)),
+            dma((4,)),
             dma((ELEMS,)),
             dma((3,)),
             dma((3,)),
@@ -420,7 +431,7 @@
             dma((6,)),
         ],
         compiler_params=pltpu.CompilerParams(
-            collective_id=0, has_side_effects=True, vmem_limit_bytes=60 * 2**20
+            collective_id=0, has_side_effects=True, vmem_limit_bytes=62_488_000
         ),
     )(
         trace[0, 0],
@@ -428,8 +439,18 @@
         matrix,
         elem_faces[0, 0].T,
         orient[0, 0].T,
-        counts,
-    )
+    )
+    cond, coarse = pl.pallas_call(
+        write_out,
+        out_shape=(
+            jax.ShapeDtypeStruct((SLOTS, ROW), F32),
+            jax.ShapeDtypeStruct((4 * OWN, COARSE), F32),
+        ),
+        in_specs=[vmem] * 2,
+        out_specs=(hbm, hbm),
+        scratch_shapes=[dma((4,))],
+        compiler_params=pltpu.CompilerParams(vmem_limit_bytes=16 * 2**20),
+    )(cond, coarse)
     return cond[None, None], coarse[None]
 
 

time: 35.6 us -> 31.4 us (0.88)
  local copies, waits for them, and re-layouts: 3.58 us -> 0 us
  between operations: 1.29 us -> 0.64 us
    unnamed x2 -> x0, local copies, waits for them, and re-layouts: 3.58 us -> none
    pallas_call x1 -> x2, Pallas kernels: 30.5 us -> 30.7 us  [the longest x1 29.7 us: body(): pl.pallas_call(lambda *refs: kernel(n_dom, *refs), out_shape=(pltpu.VMEM(...]
where the time goes in v2:
time: 31.4 us; the launch traced here: 31.3 us
  Pallas kernels  30.7 us (98%)
  between operations  0.64 us (2%)
    pallas_call x1, Pallas kernels, body(): pl.pallas_call(lambda *refs: kernel(n_dom, *refs), out_shape=(pltpu.VMEM(...  29.7 us
    pallas_call x1, Pallas kernels, body(): pl.pallas_call(write_out, out_shape=(jax.ShapeDtypeStruct((SLOTS, ROW), F...  0.93 us

profile of v2, /device:TPU:56, one launch (start us, length us, event | category | flops | bytes accessed | tf_op | source)
XLA Modules:
  0.0 31.3 jit_solution(748857976325678078)
XLA Ops:
  0.6 29.7 %shard_map.68 = (f32[80,1280]{1,0:T(8,128)S(1)}, f32[288,384]{1,0:T(8,128)S(1)}) custom-call(f32[72,1280]{1,0:T(8,128)} %bitcast.14, f32[72,1280]{1,0:T(8,128)} %bitcast.15, f32[4,200,8,128]{3,2,1,0:T(8,128)} %bitcast.13, s32[4,32]{1,0:T(4,128)} %bitcast.16, s32[4,32]{1,0:T(4,128)} %bitcast.17), custom_call_target="tpu_custom_call" | custom-call | tf_op jit(solution)/shard_map/pallas_call | solution.py:400
  30.4 0.9 %shard_map.69 = (f32[80,1280]{1,0:T(8,128)}, f32[288,384]{1,0:T(8,128)}) custom-call(f32[80,1280]{1,0:T(8,128)S(1)} %get-tuple-element.6.cond, f32[288,384]{1,0:T(8,128)S(1)} %get-tuple-element.7.coarse), custom_call_target="tpu_custom_call" | custom-call | tf_op jit(solution)/shard_map/pallas_call | solution.py:443

commit v3 on v2

--- a/solution.py
+++ b/solution.py
@@ -16,7 +16,7 @@
 SLOTS = 80
 ROW = 1280
 COARSE = 384
-HEAD = 40
+PIECE = 24
 
 NODE_LIST = [(a, b, 3 - a - b) for a in range(4) for b in range(4 - a)]
 ORDERINGS = [(0, 1, 2), (1, 2, 0), (2, 0, 1), (0, 2, 1), (2, 1, 0), (1, 0, 2)]
@@ -65,6 +65,17 @@
     back = pick.T.astype(BF16)
     back_ref[:, :128] = back
     back_ref[:, 128:] = back
+
+
+def repeat_fields(value, node, out_ref):
+    rows = value.shape[0]
+    group = iota(value.shape, 1) // 32
+    moved = [value] + [pltpu.roll(value, 32 * s, 1) for s in (1, 2, 3)]
+    for field in range(4):
+        out = moved[(3 - field) % 4]
+        for g in (2, 1, 0):
+            out = jnp.where(group == g, moved[(g - field) % 4], out)
+        out_ref[pl.ds(node * 4 + field, rows, stride=40), :] = out
 
 
 def gather_values(local_ref, pick_ref, turn_ref, pieces_ref, values_ref):
@@ -80,19 +91,11 @@
         both = dot(pick, pieces_ref[:, pair * 256 : (pair + 1) * 256])
         slabs += [both[:, :128], both[:, 128:]]
     turn = turn_ref[...]
-    group = iota((128, 128), 1) // 32
     for node in range(NODES):
-        value = oriented(turn, slabs, PERM, node)
-        moved = [value] + [pltpu.roll(value, 32 * s, 1) for s in (1, 2, 3)]
-        for field in range(4):
-            out = moved[(3 - field) % 4]
-            for g in (2, 1, 0):
-                out = jnp.where(group == g, moved[(g - field) % 4], out)
-            values_ref[pl.ds(node * 4 + field, 128, stride=40), :] = out
-
-
-def element_product(e, matrix_ref, values_ref, result_ref):
-    values = values_ref[pl.ds(e * 160, 160), :]
+        repeat_fields(oriented(turn, slabs, PERM, node), node, values_ref)
+
+
+def element_product(e, matrix_ref, values):
     lane = iota((40, 128), 1)
     group = lane // 32
     high, low = split(values[:128])
@@ -123,7 +126,7 @@
         first[0:40],
         jnp.where(group == 1, first[40:80], jnp.where(group == 2, first[80:120], first[120:160])),
     )
-    result_ref[pl.ds(e * 40, 40), :] = out + second
+    return out + second
 
 
 def scatter_results(result_ref, back_ref, turn_ref, partial_ref):
@@ -134,6 +137,43 @@
         both = [oriented(turn, slabs, INVERSE, m) for m in (2 * pair, 2 * pair + 1)]
         high, low = split(jnp.concatenate(both, axis=1))
         partial_ref[:, pair * 256 : (pair + 1) * 256] = dot(back, jnp.concatenate([high, low], axis=0))
+
+
+def add_late(trace_up, low_ref, faces, matrix_ref, pick, back, turn, values_ref, result_ref, partial_ref):
+    places = []
+    for j in range(8):
+        match = faces[...] == OWN + j
+        places.append(
+            [jnp.max(jnp.where(match, iota((4, ELEMS), dim), 0)) for dim in (1, 0)]
+        )
+    lower = back[64:SLOTS, :128]
+    named = dot(lower, jnp.ones((128, 128), BF16))[8:]
+    element = dot(lower, (iota((128, 128), 0) // 4).astype(F32).astype(BF16))[8:]
+    turns = turn[...].astype(BF16)
+    turn_j = dot(lower, turns)[8:]
+    repeat = (iota((32, 8), 0) // 4 == iota((32, 8), 1)).astype(F32).astype(BF16)
+    row = dot(repeat, element.astype(BF16)) * 4.0 + (iota((32, 128), 0) % 4).astype(F32)
+    chosen = (row == iota((32, 128), 1).astype(F32)).astype(F32).astype(BF16)
+    turn_jk = dot(chosen, turns)
+    back_jk = dot(chosen, pick[:, :128]).T.astype(BF16)[:SLOTS]
+    back_jk = jnp.concatenate([back_jk, back_jk], axis=1)
+
+    trace_up.wait_recv()
+    slabs = [
+        jnp.where(named > 0.5, low_ref[:, n * 128 : (n + 1) * 128], 0.0) for n in range(NODES)
+    ]
+    for node in range(NODES):
+        repeat_fields(oriented(turn_j, slabs, PERM, node), node, values_ref)
+    for j, (e, k) in enumerate(places):
+        face = values_ref[j * 40 : (j + 1) * 40, :]
+        whole = jnp.concatenate([face * (k == i).astype(F32) for i in range(4)], axis=0)
+        result_ref[j * 40 : (j + 1) * 40, :] = element_product(e, matrix_ref, whole)
+    slabs = [result_ref[pl.ds(n, 32, stride=NODES), :] for n in range(NODES)]
+    for pair in range(NODES // 2):
+        both = [oriented(turn_jk, slabs, INVERSE, m) for m in (2 * pair, 2 * pair + 1)]
+        high, low = split(jnp.concatenate(both, axis=1))
+        part = slice(pair * 256, (pair + 1) * 256)
+        partial_ref[:, part] += dot(back_jk, jnp.concatenate([high, low], axis=0))
 
 
 def project(rows):
@@ -157,6 +197,7 @@
     cond_ref,
     coarse_ref,
     local,
+    low_trace,
     rhs,
     matrix,
     faces,
@@ -167,6 +208,8 @@
     pieces,
     values,
     result,
+    late_values,
+    late_result,
     shared,
     arrived,
     low_out,
@@ -179,14 +222,12 @@
     low_recv,
     grp_send,
     grp_recv,
+    hello,
 ):
     d = lax.axis_index("dom")
     g = lax.axis_index("grp")
     has_below = d > 0
     has_above = d < n_dom - 1
-    right = lax.rem(g + 1, 4)
-    left = lax.rem(g + 3, 4)
-    opposite = lax.rem(g + 2, 4)
 
     loads = [
         pltpu.make_async_copy(trace_hbm, local.at[pl.ds(0, OWN)], in_sem.at[0]),
@@ -202,17 +243,15 @@
     def greet(dom, grp):
         pl.semaphore_signal(barrier, inc=1, device_id=(dom, grp), device_id_type=MESH)
 
-    greet(d, right)
-    greet(d, left)
-
     @pl.when(has_below)
     def _():
-        greet(d - 1, g)
-
-    @pl.when(has_above)
-    def _():
         for i in range(4):
-            greet(d + 1, lax.rem(g + i, 4))
+            greet(d - 1, lax.rem(g + i, 4))
+
+    @pl.when(jnp.logical_not(has_below))
+    def _():
+        for i in range(1, 4):
+            greet(d, lax.rem(g + i, 4))
 
     matrix_loads = [
         pltpu.make_async_copy(matrix_hbm.at[e // 8, :, e % 8, :], matrix.at[e], matrix_sem.at[e])
@@ -222,7 +261,9 @@
         load.start()
     loads[3].start()
 
-    pl.semaphore_wait(barrier, 2 + 4 * has_below.astype(jnp.int32) + has_above.astype(jnp.int32))
+    @pl.when(has_above)
+    def _():
+        pl.semaphore_wait(barrier, 4 + 3 * (d == 0).astype(jnp.int32))
 
     def remote(src, dst, send, recv, dom, grp):
         return pltpu.make_async_remote_copy(
@@ -235,7 +276,7 @@
         )
 
     trace_up = remote(
-        trace_hbm.at[pl.ds(INNER, 8)], local.at[pl.ds(OWN, 8)], dom_send.at[0], dom_recv.at[0], d + 1, g
+        trace_hbm.at[pl.ds(INNER, 8)], low_trace, dom_send.at[0], dom_recv.at[0], d + 1, g
     )
     part_up = remote(shared.at[0], arrived.at[0], dom_send.at[1], dom_recv.at[1], d + 1, g)
     part_down = remote(shared.at[1], arrived.at[1], dom_send.at[2], dom_recv.at[2], d - 1, g)
@@ -247,48 +288,72 @@
     @pl.when(has_above)
     def _():
         trace_up.start()
-
-    @pl.when(jnp.logical_not(has_below))
-    def _():
-        local[OWN:SLOTS, :] = jnp.zeros((8, ROW), F32)
+        for i in range(1, 4):
+            pl.semaphore_signal(
+                hello, inc=1, device_id=(d + 1, lax.rem(g + i, 4)), device_id_type=MESH
+            )
 
     loads[1].wait()
     loads[2].wait()
     build_selectors(faces, orient, pick, back, turn)
     loads[0].wait()
 
+    def all_elements():
+        gather_values(local, pick, turn, pieces, values)
+
+        def block(i, carry):
+            for q in range(8):
+                pltpu.make_async_copy(
+                    matrix_hbm.at[0, :, 0, :], matrix.at[i * 8 + q], matrix_sem.at[i * 8 + q]
+                ).wait()
+            for q in range(8):
+                e = i * 8 + q
+                result[pl.ds(e * 40, 40), :] = element_product(
+                    e, matrix, values[pl.ds(e * 160, 160), :]
+                )
+            return carry
+
+        lax.fori_loop(0, ELEMS // 8, block, 0)
+        scatter_results(result, back, turn, cond_ref)
+
+    local[OWN:SLOTS, :] = jnp.zeros((8, ROW), F32)
+    all_elements()
+
     @pl.when(has_below)
     def _():
-        trace_up.wait_recv()
-
-    gather_values(local, pick, turn, pieces, values)
-
-    def block(i, carry):
-        for q in range(8):
-            e = i * 8 + q
-            pltpu.make_async_copy(matrix_hbm.at[0, :, 0, :], matrix.at[e], matrix_sem.at[e]).wait()
-        for q in range(8):
-            element_product(i * 8 + q, matrix, values, result)
-        return carry
-
-    lax.fori_loop(0, ELEMS // 8, block, 0)
-    scatter_results(result, back, turn, cond_ref)
+        add_late(
+            trace_up,
+            low_trace,
+            faces,
+            matrix,
+            pick,
+            back,
+            turn,
+            late_values,
+            late_result,
+            cond_ref,
+        )
 
     shared[0] = cond_ref[INNER:OWN, :]
     shared[1] = cond_ref[OWN:SLOTS, :]
+
+    @pl.when(has_above)
+    def _():
+        part_up.start()
+
+    @pl.when(has_below)
+    def _():
+        part_down.start()
+
     low = project(lambda n: cond_ref[OWN:SLOTS, n * 128 : (n + 1) * 128])
     for v in range(3):
         low_out[:, v * 128 : (v + 1) * 128] = low[v]
 
     @pl.when(has_below)
     def _():
-        part_down.start()
+        pl.semaphore_wait(hello, 3)
         for copy in low_down:
             copy.start()
-
-    @pl.when(has_above)
-    def _():
-        part_up.start()
 
     loads[3].wait()
     mine = pl.multiple_of(g * OWN, 8)
@@ -300,44 +365,15 @@
     for v in range(3):
         coarse_ref[pl.ds(mine, OWN), v * 128 : (v + 1) * 128] = jnp.where(keep, own[v], 0.0)
 
-    def piece(owner, which):
-        start = pl.multiple_of(owner * OWN + HEAD * which, 8)
-        return coarse_ref.at[pl.ds(start, (HEAD, OWN - HEAD)[which])]
-
-    def pass_on(owner, which, number, to):
-        return remote(
-            piece(owner, which),
-            piece(owner, which),
-            grp_send.at[number],
-            grp_recv.at[number],
-            d,
-            to,
-        )
-
-    sends = [
-        pass_on(g, 0, 0, right),
-        pass_on(g, 1, 1, left),
-        pass_on(g, 1, 2, right),
-        pass_on(g, 0, 3, left),
-    ]
+    def message(owner, i, n):
+        rows = coarse_ref.at[pl.ds(pl.multiple_of(owner * OWN + PIECE * n, 8), PIECE)]
+        number = 3 * (i - 1) + n
+        to = lax.rem(g + i, 4)
+        return remote(rows, rows, grp_send.at[number], grp_recv.at[number], d, to)
+
+    sends = [message(g, i, n) for n in range(OWN // PIECE) for i in (2, 1, 3)]
     for copy in sends:
         copy.start()
-    onward = [pass_on(left, 0, 4, right), pass_on(right, 1, 5, left)]
-
-    def arrival(owner, which, number):
-        return remote(
-            piece(owner, which),
-            piece(owner, which),
-            grp_send.at[number],
-            grp_recv.at[number],
-            d,
-            right,
-        )
-
-    arrival(left, 0, 0).wait_recv()
-    onward[0].start()
-    arrival(right, 1, 1).wait_recv()
-    onward[1].start()
 
     @pl.when(has_above)
     def _():
@@ -349,14 +385,11 @@
         part_up.wait_recv()
         cond_ref[OWN:SLOTS, :] = shared[1] + arrived[0]
 
-    arrival(left, 1, 2).wait_recv()
-    arrival(right, 0, 3).wait_recv()
     for copy in sends:
         copy.wait_send()
-    for copy in onward:
-        copy.wait_send()
-    arrival(opposite, 0, 4).wait_recv()
-    arrival(opposite, 1, 5).wait_recv()
+    for i in range(1, 4):
+        for n in range(OWN // PIECE):
+            message(lax.rem(g + 4 - i, 4), i, n).wait_recv()
 
     @pl.when(has_above)
     def _():
@@ -407,6 +440,7 @@
         out_specs=(vmem, vmem),
         scratch_shapes=[
             pltpu.VMEM((SLOTS, ROW), F32),
+            pltpu.VMEM((8, ROW), F32),
             pltpu.VMEM((OWN, ROW), F32),
             pltpu.VMEM((ELEMS, 200, 128), F32),
             pltpu.VMEM((4, ELEMS), jnp.int32),
@@ -417,6 +451,8 @@
             pltpu.VMEM((256, ROW), BF16),
             pltpu.VMEM((ELEMS * 160, 128), F32),
             pltpu.VMEM((ELEMS * 40, 128), F32),
+            pltpu.VMEM((8 * 40, 128), F32),
+            pltpu.VMEM((8 * 40, 128), F32),
             pltpu.VMEM((2, 8, ROW), F32),
             pltpu.VMEM((2, 8, ROW), F32),
             pltpu.VMEM((8, COARSE), F32),
@@ -427,8 +463,9 @@
             dma((3,)),
             dma((4,)),
             dma((4,)),
-            dma((6,)),
-            dma((6,)),
+            dma((9,)),
+            dma((9,)),
+            pltpu.SemaphoreType.REGULAR,
         ],
         compiler_params=pltpu.CompilerParams(
             collective_id=0, has_side_effects=True, vmem_limit_bytes=62_488_000

time: 31.4 us -> 25.8 us (0.82)
  Pallas kernels: 30.7 us -> 25 us
    pallas_call x1, Pallas kernels: 29.7 us -> 24 us  [body(): pl.pallas_call(lambda *refs: kernel(n_dom, *refs), out_shape=(pltpu.VMEM(...]
where the time goes in v3:
time: 25.8 us; the launch traced here: 25.6 us
  Pallas kernels  25 us (97%)
  between operations  0.64 us (2%)
    pallas_call x1, Pallas kernels, body(): pl.pallas_call(lambda *refs: kernel(n_dom, *refs), out_shape=(pltpu.VMEM(...  24 us
    pallas_call x1, Pallas kernels, body(): pl.pallas_call(write_out, out_shape=(jax.ShapeDtypeStruct((SLOTS, ROW), F...  0.93 us

profile of v3, /device:TPU:56, one launch (start us, length us, event | category | flops | bytes accessed | tf_op | source)
XLA Modules:
  0.0 25.6 jit_solution(2064615743957208630)
XLA Ops:
  0.6 24.0 %shard_map.68 = (f32[80,1280]{1,0:T(8,128)S(1)}, f32[288,384]{1,0:T(8,128)S(1)}) custom-call(f32[72,1280]{1,0:T(8,128)} %bitcast.14, f32[72,1280]{1,0:T(8,128)} %bitcast.15, f32[4,200,8,128]{3,2,1,0:T(8,128)} %bitcast.13, s32[4,32]{1,0:T(4,128)} %bitcast.16, s32[4,32]{1,0:T(4,128)} %bitcast.17), custom_call_target="tpu_custom_call" | custom-call | tf_op jit(solution)/shard_map/pallas_call | solution.py:433
  24.7 0.9 %shard_map.69 = (f32[80,1280]{1,0:T(8,128)}, f32[288,384]{1,0:T(8,128)}) custom-call(f32[80,1280]{1,0:T(8,128)S(1)} %get-tuple-element.6.cond, f32[288,384]{1,0:T(8,128)S(1)} %get-tuple-element.7.coarse), custom_call_target="tpu_custom_call" | custom-call | tf_op jit(solution)/shard_map/pallas_call | solution.py:480

commit v4 on v3

--- a/solution.py
+++ b/solution.py
@@ -16,6 +16,7 @@
 SLOTS = 80
 ROW = 1280
 COARSE = 384
+ROW_LENGTH = 24
 PIECE = 24
 
 NODE_LIST = [(a, b, 3 - a - b) for a in range(4) for b in range(4 - a)]
@@ -139,26 +140,27 @@
         partial_ref[:, pair * 256 : (pair + 1) * 256] = dot(back, jnp.concatenate([high, low], axis=0))
 
 
-def add_late(trace_up, low_ref, faces, matrix_ref, pick, back, turn, values_ref, result_ref, partial_ref):
+def prepare_late(faces, pick, back, turn):
     places = []
     for j in range(8):
         match = faces[...] == OWN + j
-        places.append(
-            [jnp.max(jnp.where(match, iota((4, ELEMS), dim), 0)) for dim in (1, 0)]
-        )
+        places.append([jnp.max(jnp.where(match, iota((4, ELEMS), dim), 0)) for dim in (1, 0)])
     lower = back[64:SLOTS, :128]
     named = dot(lower, jnp.ones((128, 128), BF16))[8:]
     element = dot(lower, (iota((128, 128), 0) // 4).astype(F32).astype(BF16))[8:]
     turns = turn[...].astype(BF16)
     turn_j = dot(lower, turns)[8:]
-    repeat = (iota((32, 8), 0) // 4 == iota((32, 8), 1)).astype(F32).astype(BF16)
-    row = dot(repeat, element.astype(BF16)) * 4.0 + (iota((32, 128), 0) % 4).astype(F32)
-    chosen = (row == iota((32, 128), 1).astype(F32)).astype(F32).astype(BF16)
-    turn_jk = dot(chosen, turns)
-    back_jk = dot(chosen, pick[:, :128]).T.astype(BF16)[:SLOTS]
-    back_jk = jnp.concatenate([back_jk, back_jk], axis=1)
-
-    trace_up.wait_recv()
+    repeat = (iota((128, 8), 0) % 32 // 4 == iota((128, 8), 1)).astype(F32).astype(BF16)
+    row = dot(repeat, element.astype(BF16)) * 4.0 + (iota((128, 128), 0) % 4).astype(F32)
+    chosen = (row == iota((128, 128), 1).astype(F32)).astype(F32).astype(BF16)
+    turn_jk = dot(chosen, turns)[:32]
+    back_jk = dot(chosen, pick[:, :128]).T.astype(BF16)
+    slots = dot(iota((8, 128), 1).astype(F32).astype(BF16), back_jk)
+    slots = jnp.where(iota((8, 128), 1) < 64, slots, -1.0)
+    return places, named, turn_j, turn_jk, back_jk[:SLOTS, :64], slots
+
+
+def late_products(places, named, turn_j, turn_jk, low_ref, matrix_ref, values_ref, result_ref, rows_ref):
     slabs = [
         jnp.where(named > 0.5, low_ref[:, n * 128 : (n + 1) * 128], 0.0) for n in range(NODES)
     ]
@@ -169,10 +171,14 @@
         whole = jnp.concatenate([face * (k == i).astype(F32) for i in range(4)], axis=0)
         result_ref[j * 40 : (j + 1) * 40, :] = element_product(e, matrix_ref, whole)
     slabs = [result_ref[pl.ds(n, 32, stride=NODES), :] for n in range(NODES)]
+    for node in range(NODES):
+        rows_ref[:, node * 128 : (node + 1) * 128] = oriented(turn_jk, slabs, INVERSE, node)
+
+
+def add_rows(back_jk, rows_ref, partial_ref):
     for pair in range(NODES // 2):
-        both = [oriented(turn_jk, slabs, INVERSE, m) for m in (2 * pair, 2 * pair + 1)]
-        high, low = split(jnp.concatenate(both, axis=1))
         part = slice(pair * 256, (pair + 1) * 256)
+        high, low = split(rows_ref[:, part])
         partial_ref[:, part] += dot(back_jk, jnp.concatenate([high, low], axis=0))
 
 
@@ -210,6 +216,9 @@
     result,
     late_values,
     late_result,
+    late_rows,
+    slots,
+    extra,
     shared,
     arrived,
     low_out,
@@ -223,6 +232,11 @@
     grp_send,
     grp_recv,
     hello,
+    hello_back,
+    slot_send,
+    slot_recv,
+    extra_send,
+    extra_recv,
 ):
     d = lax.axis_index("dom")
     g = lax.axis_index("grp")
@@ -257,10 +271,6 @@
         pltpu.make_async_copy(matrix_hbm.at[e // 8, :, e % 8, :], matrix.at[e], matrix_sem.at[e])
         for e in range(ELEMS)
     ]
-    for load in matrix_loads:
-        load.start()
-    loads[3].start()
-
     @pl.when(has_above)
     def _():
         pl.semaphore_wait(barrier, 4 + 3 * (d == 0).astype(jnp.int32))
@@ -293,6 +303,9 @@
                 hello, inc=1, device_id=(d + 1, lax.rem(g + i, 4)), device_id_type=MESH
             )
 
+    for load in matrix_loads:
+        load.start()
+    loads[3].start()
     loads[1].wait()
     loads[2].wait()
     build_selectors(faces, orient, pick, back, turn)
@@ -318,52 +331,17 @@
 
     local[OWN:SLOTS, :] = jnp.zeros((8, ROW), F32)
     all_elements()
-
-    @pl.when(has_below)
-    def _():
-        add_late(
-            trace_up,
-            low_trace,
-            faces,
-            matrix,
-            pick,
-            back,
-            turn,
-            late_values,
-            late_result,
-            cond_ref,
-        )
-
-    shared[0] = cond_ref[INNER:OWN, :]
-    shared[1] = cond_ref[OWN:SLOTS, :]
-
-    @pl.when(has_above)
-    def _():
-        part_up.start()
-
-    @pl.when(has_below)
-    def _():
-        part_down.start()
-
-    low = project(lambda n: cond_ref[OWN:SLOTS, n * 128 : (n + 1) * 128])
-    for v in range(3):
-        low_out[:, v * 128 : (v + 1) * 128] = low[v]
-
-    @pl.when(has_below)
-    def _():
-        pl.semaphore_wait(hello, 3)
-        for copy in low_down:
-            copy.start()
-
     loads[3].wait()
     mine = pl.multiple_of(g * OWN, 8)
-    own = project(
-        lambda n: rhs[:, n * 128 : (n + 1) * 128] - cond_ref[0:OWN, n * 128 : (n + 1) * 128]
-    )
-    named = dot(back[0:SLOTS, :128], jnp.ones((128, 128), BF16))[:OWN]
-    keep = jnp.logical_or(iota((OWN, 128), 0) < INNER, named > 0.5)
-    for v in range(3):
-        coarse_ref[pl.ds(mine, OWN), v * 128 : (v + 1) * 128] = jnp.where(keep, own[v], 0.0)
+
+    def own_coarse():
+        own = project(
+            lambda n: rhs[:, n * 128 : (n + 1) * 128] - cond_ref[0:OWN, n * 128 : (n + 1) * 128]
+        )
+        named = dot(back[0:SLOTS, :128], jnp.ones((128, 128), BF16))[:OWN]
+        keep = jnp.logical_or(iota((OWN, 128), 0) < INNER, named > 0.5)
+        for v in range(3):
+            coarse_ref[pl.ds(mine, OWN), v * 128 : (v + 1) * 128] = jnp.where(keep, own[v], 0.0)
 
     def message(owner, i, n):
         rows = coarse_ref.at[pl.ds(pl.multiple_of(owner * OWN + PIECE * n, 8), PIECE)]
@@ -371,9 +349,83 @@
         to = lax.rem(g + i, 4)
         return remote(rows, rows, grp_send.at[number], grp_recv.at[number], d, to)
 
+    def to_peer(array, send, recv, i):
+        return remote(
+            array.at[0], array.at[i], send.at[i - 1], recv.at[i - 1], d, lax.rem(g + i, 4)
+        )
+
     sends = [message(g, i, n) for n in range(OWN // PIECE) for i in (2, 1, 3)]
-    for copy in sends:
-        copy.start()
+    slot_sends = [to_peer(slots, slot_send, slot_recv, i) for i in (2, 1, 3)]
+    extra_sends = [to_peer(extra, extra_send, extra_recv, i) for i in (2, 1, 3)]
+
+    place = lax.rem(d, ROW_LENGTH)
+    ahead = jnp.logical_and(place == 0, has_below)
+    after_ahead = jnp.logical_and(place == 1, d > 1)
+
+    @pl.when(has_below)
+    def _():
+        places, named, turn_j, turn_jk, back_jk, slot_row = prepare_late(faces, pick, back, turn)
+
+        @pl.when(ahead)
+        def _():
+            own_coarse()
+            slots[0] = slot_row
+            pl.semaphore_wait(hello_back, 1)
+            for copy in sends:
+                copy.start()
+            for copy in slot_sends:
+                copy.start()
+
+        trace_up.wait_recv()
+
+        @pl.when(after_ahead)
+        def _():
+            pl.semaphore_wait(hello, 3)
+            pl.semaphore_signal(hello_back, inc=1, device_id=(d - 1, g), device_id_type=MESH)
+
+        late_products(
+            places, named, turn_j, turn_jk, low_trace, matrix, late_values, late_result, late_rows
+        )
+
+        @pl.when(ahead)
+        def _():
+            more = project(lambda n: late_rows[:, n * 128 : (n + 1) * 128])
+            for v in range(3):
+                extra[0, :, v * 128 : (v + 1) * 128] = more[v]
+            for copy in extra_sends:
+                copy.start()
+
+        add_rows(back_jk, late_rows, cond_ref)
+
+    shared[0] = cond_ref[INNER:OWN, :]
+    shared[1] = cond_ref[OWN:SLOTS, :]
+
+    @pl.when(has_above)
+    def _():
+        part_up.start()
+
+    @pl.when(has_below)
+    def _():
+        part_down.start()
+
+    low = project(lambda n: cond_ref[OWN:SLOTS, n * 128 : (n + 1) * 128])
+    for v in range(3):
+        low_out[:, v * 128 : (v + 1) * 128] = low[v]
+
+    @pl.when(has_below)
+    def _():
+        @pl.when(jnp.logical_not(after_ahead))
+        def _():
+            pl.semaphore_wait(hello, 3)
+
+        for copy in low_down:
+            copy.start()
+
+    @pl.when(jnp.logical_not(ahead))
+    def _():
+        own_coarse()
+        for copy in sends:
+            copy.start()
 
     @pl.when(has_above)
     def _():
@@ -390,6 +442,19 @@
     for i in range(1, 4):
         for n in range(OWN // PIECE):
             message(lax.rem(g + 4 - i, 4), i, n).wait_recv()
+
+    @pl.when(ahead)
+    def _():
+        for copy in slot_sends + extra_sends:
+            copy.wait()
+        for i in range(4):
+            rows = pl.ds(pl.multiple_of(lax.rem(g + 4 - i, 4) * OWN, 8), OWN)
+            target = iota((OWN, 128), 0).astype(F32) == slots[i, 0:1, :]
+            high, low = split(extra[i])
+            more = dot(
+                target.astype(F32).astype(BF16)[:, :64], jnp.concatenate([high, low], axis=0)
+            )
+            coarse_ref[rows, :] = coarse_ref[rows, :] - more
 
     @pl.when(has_above)
     def _():
@@ -453,6 +518,9 @@
             pltpu.VMEM((ELEMS * 40, 128), F32),
             pltpu.VMEM((8 * 40, 128), F32),
             pltpu.VMEM((8 * 40, 128), F32),
+            pltpu.VMEM((32, ROW), F32),
+            pltpu.VMEM((4, 8, 128), F32),
+            pltpu.VMEM((4, 32, COARSE), F32),
             pltpu.VMEM((2, 8, ROW), F32),
             pltpu.VMEM((2, 8, ROW), F32),
             pltpu.VMEM((8, COARSE), F32),
@@ -466,6 +534,11 @@
             dma((9,)),
             dma((9,)),
             pltpu.SemaphoreType.REGULAR,
+            pltpu.SemaphoreType.REGULAR,
+            dma((3,)),
+            dma((3,)),
+            dma((3,)),
+            dma((3,)),
         ],
         compiler_params=pltpu.CompilerParams(
             collective_id=0, has_side_effects=True, vmem_limit_bytes=62_488_000

time: 25.8 us -> 24.3 us (0.942)
  Pallas kernels: 25 us -> 23.5 us
    pallas_call x1, Pallas kernels: 24 us -> 22.6 us  [body(): pl.pallas_call(lambda *refs: kernel(n_dom, *refs), out_shape=(pltpu.VMEM(...]
where the time goes in v4:
time: 24.3 us; the launch traced here: 24.2 us
  Pallas kernels  23.5 us (97%)
  between operations  0.64 us (3%)
    pallas_call x1, Pallas kernels, body(): pl.pallas_call(lambda *refs: kernel(n_dom, *refs), out_shape=(pltpu.VMEM(...  22.6 us
    pallas_call x1, Pallas kernels, body(): pl.pallas_call(write_out, out_shape=(jax.ShapeDtypeStruct((SLOTS, ROW), F...  0.93 us

profile of v4, /device:TPU:56, one launch (start us, length us, event | category | flops | bytes accessed | tf_op | source)
XLA Modules:
  0.0 24.2 jit_solution(14184870349622758196)
XLA Ops:
  0.6 22.6 %shard_map.68 = (f32[80,1280]{1,0:T(8,128)S(1)}, f32[288,384]{1,0:T(8,128)S(1)}) custom-call(f32[72,1280]{1,0:T(8,128)} %bitcast.14, f32[72,1280]{1,0:T(8,128)} %bitcast.15, f32[4,200,8,128]{3,2,1,0:T(8,128)} %bitcast.13, s32[4,32]{1,0:T(4,128)} %bitcast.16, s32[4,32]{1,0:T(4,128)} %bitcast.17), custom_call_target="tpu_custom_call" | custom-call | tf_op jit(solution)/shard_map/pallas_call | solution.py:498
  23.2 0.9 %shard_map.69 = (f32[80,1280]{1,0:T(8,128)}, f32[288,384]{1,0:T(8,128)}) custom-call(f32[80,1280]{1,0:T(8,128)S(1)} %get-tuple-element.6.cond, f32[288,384]{1,0:T(8,128)S(1)} %get-tuple-element.7.coarse), custom_call_target="tpu_custom_call" | custom-call | tf_op jit(solution)/shard_map/pallas_call | solution.py:553

commit v5 on v4

--- a/solution.py
+++ b/solution.py
@@ -96,38 +96,53 @@
         repeat_fields(oriented(turn, slabs, PERM, node), node, values_ref)
 
 
-def element_product(e, matrix_ref, values):
+def matrix_pieces(e, matrix_ref):
     lane = iota((40, 128), 1)
     group = lane // 32
-    high, low = split(values[:128])
-    main = jnp.concatenate([high, low], axis=1)
-    main = jnp.concatenate([main, main], axis=0)
-    last = values[128:160]
-    group32 = iota((32, 128), 1) // 32
-    rest = jnp.concatenate([jnp.where(group32 == b, last, 0.0) for b in range(4)], axis=0)
-    high, low = split(rest)
-    rest = jnp.concatenate([high, low], axis=1)
-    rest = jnp.concatenate([rest, rest], axis=0)
     parts = [matrix_ref[e, pl.ds(c, 40, stride=5), :] for c in range(5)]
     rows = [parts[0]]
     for b in range(1, 4):
         mixed = jnp.where(lane >= 32 * b, parts[b], parts[b + 1])
         rows.append(pltpu.roll(mixed, 128 - 32 * b, 1))
     high, low = split(jnp.concatenate(rows, axis=0))
-    first = dot(jnp.concatenate([high, low], axis=1), main)
+    main = jnp.concatenate([high, low], axis=1)
     tail = jnp.where(
         group == 0, parts[1], jnp.where(group == 1, parts[2], jnp.where(group == 2, parts[3], parts[4]))
     )
-    high, low = split(tail)
-    second = dot(jnp.concatenate([high, low], axis=1), rest)
+    return main, tail
+
+
+def value_pieces(values):
+    high, low = split(values[:128])
+    main = jnp.concatenate([high, low], axis=1)
+    main = jnp.concatenate([main, main], axis=0)
+    last = values[128:160]
+    group = iota((32, 128), 1) // 32
+    rest = jnp.concatenate([jnp.where(group == b, last, 0.0) for b in range(4)], axis=0)
+    high, low = split(rest)
+    rest = jnp.concatenate([high, low], axis=1)
+    return main, jnp.concatenate([rest, rest], axis=0)
+
+
+def pieces_product(matrix_main, matrix_tail, values):
+    main, rest = value_pieces(values)
+    first = dot(matrix_main, main)
+    second = dot(matrix_tail, rest)[:40]
     first = first[:, :128] + first[:, 128:]
     second = second[:, :128] + second[:, 128:]
+    group = iota((40, 128), 1) // 32
     out = jnp.where(
         group == 0,
         first[0:40],
         jnp.where(group == 1, first[40:80], jnp.where(group == 2, first[80:120], first[120:160])),
     )
     return out + second
+
+
+def element_product(e, matrix_ref, values):
+    main, tail = matrix_pieces(e, matrix_ref)
+    high, low = split(tail)
+    return pieces_product(main, jnp.concatenate([high, low], axis=1), values)
 
 
 def scatter_results(result_ref, back_ref, turn_ref, partial_ref):
@@ -140,16 +155,18 @@
         partial_ref[:, pair * 256 : (pair + 1) * 256] = dot(back, jnp.concatenate([high, low], axis=0))
 
 
-def prepare_late(faces, pick, back, turn):
+def prepare_late(faces, pick, back, turn, start):
     places = []
     for j in range(8):
-        match = faces[...] == OWN + j
+        match = faces[...] == start + j
         places.append([jnp.max(jnp.where(match, iota((4, ELEMS), dim), 0)) for dim in (1, 0)])
     lower = back[64:SLOTS, :128]
-    named = dot(lower, jnp.ones((128, 128), BF16))[8:]
-    element = dot(lower, (iota((128, 128), 0) // 4).astype(F32).astype(BF16))[8:]
+    part = slice(start - 64, start - 56)
+    named = dot(lower, jnp.ones((128, 128), BF16))[part]
+    element = dot(lower, (iota((128, 128), 0) // 4).astype(F32).astype(BF16))[part]
+    face = dot(lower, (iota((128, 128), 0) % 4).astype(F32).astype(BF16))[part]
     turns = turn[...].astype(BF16)
-    turn_j = dot(lower, turns)[8:]
+    turn_j = dot(lower, turns)[part]
     repeat = (iota((128, 8), 0) % 32 // 4 == iota((128, 8), 1)).astype(F32).astype(BF16)
     row = dot(repeat, element.astype(BF16)) * 4.0 + (iota((128, 128), 0) % 4).astype(F32)
     chosen = (row == iota((128, 128), 1).astype(F32)).astype(F32).astype(BF16)
@@ -157,10 +174,33 @@
     back_jk = dot(chosen, pick[:, :128]).T.astype(BF16)
     slots = dot(iota((8, 128), 1).astype(F32).astype(BF16), back_jk)
     slots = jnp.where(iota((8, 128), 1) < 64, slots, -1.0)
-    return places, named, turn_j, turn_jk, back_jk[:SLOTS, :64], slots
-
-
-def late_products(places, named, turn_j, turn_jk, low_ref, matrix_ref, values_ref, result_ref, rows_ref):
+    return places, named, face, turn_j, turn_jk, back_jk[:SLOTS, :64], slots
+
+
+def owned_products(places, named, face, turn_jk, matrix_ref, values_ref, result_ref, rows_ref, out_ref):
+    for j, (e, k) in enumerate(places):
+        values = values_ref[pl.ds(e * 160, 160), :]
+        result_ref[j * 40 : (j + 1) * 40, :] = element_product(e, matrix_ref, values)
+    late_to_slots(turn_jk, result_ref, rows_ref)
+    lane = iota((8, 128), 1) % 32
+    own = jnp.logical_and(lane // 4 == iota((8, 128), 0), (lane % 4).astype(F32) == face)
+    own = jnp.where(jnp.logical_and(own, named > 0.5), 1.0, 0.0)
+    own = jnp.concatenate([own, jnp.zeros((8, 128), F32)], axis=0).astype(BF16)[:, :64]
+    for pair in range(NODES // 2):
+        part = slice(pair * 256, (pair + 1) * 256)
+        high, low = split(rows_ref[:, part])
+        out_ref[:, part] = dot(own, jnp.concatenate([high, low], axis=0))[:8]
+
+
+def prepare_matrices(places, matrix_ref, ready_ref):
+    for j, (e, k) in enumerate(places):
+        main, tail = matrix_pieces(e, matrix_ref)
+        high, low = split(jnp.concatenate([tail, jnp.zeros((8, 128), F32)], axis=0))
+        ready_ref[j, 0:160, :] = main
+        ready_ref[j, 160:208, :] = jnp.concatenate([high, low], axis=1)
+
+
+def late_products(places, named, turn_j, low_ref, ready_ref, values_ref, result_ref):
     slabs = [
         jnp.where(named > 0.5, low_ref[:, n * 128 : (n + 1) * 128], 0.0) for n in range(NODES)
     ]
@@ -169,17 +209,36 @@
     for j, (e, k) in enumerate(places):
         face = values_ref[j * 40 : (j + 1) * 40, :]
         whole = jnp.concatenate([face * (k == i).astype(F32) for i in range(4)], axis=0)
-        result_ref[j * 40 : (j + 1) * 40, :] = element_product(e, matrix_ref, whole)
+        result_ref[j * 40 : (j + 1) * 40, :] = pieces_product(
+            ready_ref[j, 0:160, :], ready_ref[j, 160:208, :], whole
+        )
+
+
+def late_to_slots(turn_jk, result_ref, rows_ref):
     slabs = [result_ref[pl.ds(n, 32, stride=NODES), :] for n in range(NODES)]
     for node in range(NODES):
         rows_ref[:, node * 128 : (node + 1) * 128] = oriented(turn_jk, slabs, INVERSE, node)
 
 
-def add_rows(back_jk, rows_ref, partial_ref):
+def add_rows(back_jk, rows_ref, partial_ref, start, stop):
     for pair in range(NODES // 2):
         part = slice(pair * 256, (pair + 1) * 256)
         high, low = split(rows_ref[:, part])
-        partial_ref[:, part] += dot(back_jk, jnp.concatenate([high, low], axis=0))
+        partial_ref[start:stop, part] += dot(
+            back_jk[start:stop], jnp.concatenate([high, low], axis=0)
+        )
+
+
+def project_late(turn_jk, result_ref):
+    slabs = [result_ref[pl.ds(n, 32, stride=NODES), :] for n in range(NODES)]
+    corners = project(lambda n: slabs[n])
+    out = []
+    for v in range(3):
+        row = corners[ORDERINGS[5][v]]
+        for o in range(4, -1, -1):
+            row = jnp.where(turn_jk == o, corners[ORDERINGS[o][v]], row)
+        out.append(row)
+    return out
 
 
 def project(rows):
@@ -217,6 +276,8 @@
     late_values,
     late_result,
     late_rows,
+    early,
+    ready,
     slots,
     extra,
     shared,
@@ -303,22 +364,57 @@
                 hello, inc=1, device_id=(d + 1, lax.rem(g + i, 4)), device_id_type=MESH
             )
 
-    for load in matrix_loads:
+    for load in matrix_loads + loads[3:]:
         load.start()
-    loads[3].start()
     loads[1].wait()
     loads[2].wait()
     build_selectors(faces, orient, pick, back, turn)
     loads[0].wait()
 
+    place = lax.rem(d, ROW_LENGTH)
+    ahead = jnp.logical_and(place == 0, has_below)
+    after_ahead = jnp.logical_and(place == 1, d > 1)
+    tail = jnp.logical_and(place == ROW_LENGTH - 1, has_above)
+    not_tail = jnp.logical_not(tail)
+
+    def late_part(ready_late):
+        places, named, face, turn_j, turn_jk, back_jk, slot_row = ready_late
+        prepare_matrices(places, matrix, ready)
+        trace_up.wait_recv()
+        late_products(places, named, turn_j, low_trace, ready, late_values, late_result)
+
+    def owned_first():
+        for load in matrix_loads:
+            load.wait()
+        places, named, face, turn_j, turn_jk, back_jk, slot_row = prepare_late(
+            faces, pick, back, turn, INNER
+        )
+        owned_products(
+            places, named, face, turn_jk, matrix, values, late_result, late_rows, early
+        )
+        ready_late = prepare_late(faces, pick, back, turn, OWN)
+        late_part(ready_late)
+        late_to_slots(ready_late[4], late_result, late_rows)
+        back_jk = ready_late[5][INNER:SLOTS]
+        for pair in range(NODES // 2):
+            part = slice(pair * 256, (pair + 1) * 256)
+            high, low = split(late_rows[:, part])
+            more = dot(back_jk, jnp.concatenate([high, low], axis=0))[:8]
+            shared[0, :, part] = early[:, part] + more
+        part_up.start()
+
     def all_elements():
         gather_values(local, pick, turn, pieces, values)
+        pl.when(tail)(owned_first)
 
         def block(i, carry):
-            for q in range(8):
-                pltpu.make_async_copy(
-                    matrix_hbm.at[0, :, 0, :], matrix.at[i * 8 + q], matrix_sem.at[i * 8 + q]
-                ).wait()
+            @pl.when(not_tail)
+            def _():
+                for q in range(8):
+                    pltpu.make_async_copy(
+                        matrix_hbm.at[0, :, 0, :], matrix.at[i * 8 + q], matrix_sem.at[i * 8 + q]
+                    ).wait()
+
             for q in range(8):
                 e = i * 8 + q
                 result[pl.ds(e * 40, 40), :] = element_product(
@@ -356,15 +452,24 @@
 
     sends = [message(g, i, n) for n in range(OWN // PIECE) for i in (2, 1, 3)]
     slot_sends = [to_peer(slots, slot_send, slot_recv, i) for i in (2, 1, 3)]
-    extra_sends = [to_peer(extra, extra_send, extra_recv, i) for i in (2, 1, 3)]
-
-    place = lax.rem(d, ROW_LENGTH)
-    ahead = jnp.logical_and(place == 0, has_below)
-    after_ahead = jnp.logical_and(place == 1, d > 1)
+    extra_sends = [to_peer(extra, extra_send, extra_recv, i) for i in (1, 2, 3)]
+
+    def send_parts():
+        shared[1] = cond_ref[OWN:SLOTS, :]
+
+        @pl.when(jnp.logical_and(has_above, not_tail))
+        def _():
+            shared[0] = cond_ref[INNER:OWN, :]
+            part_up.start()
+
+        @pl.when(has_below)
+        def _():
+            part_down.start()
 
     @pl.when(has_below)
     def _():
-        places, named, turn_j, turn_jk, back_jk, slot_row = prepare_late(faces, pick, back, turn)
+        ready_late = prepare_late(faces, pick, back, turn, OWN)
+        places, named, face, turn_j, turn_jk, back_jk, slot_row = ready_late
 
         @pl.when(ahead)
         def _():
@@ -376,37 +481,31 @@
             for copy in slot_sends:
                 copy.start()
 
-        trace_up.wait_recv()
+        @pl.when(not_tail)
+        def _():
+            late_part(ready_late)
 
         @pl.when(after_ahead)
         def _():
             pl.semaphore_wait(hello, 3)
             pl.semaphore_signal(hello_back, inc=1, device_id=(d - 1, g), device_id_type=MESH)
 
-        late_products(
-            places, named, turn_j, turn_jk, low_trace, matrix, late_values, late_result, late_rows
-        )
-
         @pl.when(ahead)
         def _():
-            more = project(lambda n: late_rows[:, n * 128 : (n + 1) * 128])
+            more = project_late(turn_jk, late_result)
             for v in range(3):
                 extra[0, :, v * 128 : (v + 1) * 128] = more[v]
             for copy in extra_sends:
                 copy.start()
 
-        add_rows(back_jk, late_rows, cond_ref)
-
-    shared[0] = cond_ref[INNER:OWN, :]
-    shared[1] = cond_ref[OWN:SLOTS, :]
-
-    @pl.when(has_above)
-    def _():
-        part_up.start()
-
-    @pl.when(has_below)
-    def _():
-        part_down.start()
+        late_to_slots(turn_jk, late_result, late_rows)
+        add_rows(back_jk, late_rows, cond_ref, INNER, SLOTS)
+        send_parts()
+        add_rows(back_jk, late_rows, cond_ref, 0, INNER)
+
+    @pl.when(jnp.logical_not(has_below))
+    def _():
+        send_parts()
 
     low = project(lambda n: cond_ref[OWN:SLOTS, n * 128 : (n + 1) * 128])
     for v in range(3):
@@ -443,11 +542,21 @@
         for n in range(OWN // PIECE):
             message(lax.rem(g + 4 - i, 4), i, n).wait_recv()
 
+    @pl.when(has_above)
+    def _():
+        for i in range(4):
+            low_down[i].wait_recv()
+            owner = lax.rem(g + 4 - i, 4)
+            rows = pl.ds(pl.multiple_of(owner * OWN + INNER, 8), 8)
+            coarse_ref[rows, :] = coarse_ref[rows, :] - low_in[i]
+
     @pl.when(ahead)
     def _():
-        for copy in slot_sends + extra_sends:
+        for copy in slot_sends:
             copy.wait()
-        for i in range(4):
+        for i in (0, 3, 2, 1):
+            if i:
+                to_peer(extra, extra_send, extra_recv, i).wait_recv()
             rows = pl.ds(pl.multiple_of(lax.rem(g + 4 - i, 4) * OWN, 8), OWN)
             target = iota((OWN, 128), 0).astype(F32) == slots[i, 0:1, :]
             high, low = split(extra[i])
@@ -455,14 +564,8 @@
                 target.astype(F32).astype(BF16)[:, :64], jnp.concatenate([high, low], axis=0)
             )
             coarse_ref[rows, :] = coarse_ref[rows, :] - more
-
-    @pl.when(has_above)
-    def _():
-        for i in range(4):
-            low_down[i].wait_recv()
-            owner = lax.rem(g + 4 - i, 4)
-            rows = pl.ds(pl.multiple_of(owner * OWN + INNER, 8), 8)
-            coarse_ref[rows, :] = coarse_ref[rows, :] - low_in[i]
+        for copy in extra_sends:
+            copy.wait_send()
 
     @pl.when(has_above)
     def _():
@@ -519,6 +622,8 @@
             pltpu.VMEM((8 * 40, 128), F32),
             pltpu.VMEM((8 * 40, 128), F32),
             pltpu.VMEM((32, ROW), F32),
+            pltpu.VMEM((8, ROW), F32),
+            pltpu.VMEM((8, 208, 256), BF16),
             pltpu.VMEM((4, 8, 128), F32),
             pltpu.VMEM((4, 32, COARSE), F32),
             pltpu.VMEM((2, 8, ROW), F32),

time: 24.3 us -> 24.6 us (1.012)
  Pallas kernels: 23.5 us -> 23.8 us
    pallas_call x1, Pallas kernels: 22.6 us -> 22.9 us  [body(): pl.pallas_call(lambda *refs: kernel(n_dom, *refs), out_shape=(pltpu.VMEM(...]
where the time goes in v5:
time: 24.6 us; the launch traced here: 24.5 us
  Pallas kernels  23.8 us (97%)
  between operations  0.64 us (3%)
    pallas_call x1, Pallas kernels, body(): pl.pallas_call(lambda *refs: kernel(n_dom, *refs), out_shape=(pltpu.VMEM(...  22.9 us
    pallas_call x1, Pallas kernels, body(): pl.pallas_call(write_out, out_shape=(jax.ShapeDtypeStruct((SLOTS, ROW), F...  0.93 us

profile of v5, /device:TPU:56, one launch (start us, length us, event | category | flops | bytes accessed | tf_op | source)
XLA Modules:
  0.0 24.5 jit_solution(4681974071196404623)
XLA Ops:
  0.6 22.9 %shard_map.68 = (f32[80,1280]{1,0:T(8,128)S(1)}, f32[288,384]{1,0:T(8,128)S(1)}) custom-call(f32[72,1280]{1,0:T(8,128)} %bitcast.14, f32[72,1280]{1,0:T(8,128)} %bitcast.15, f32[4,200,8,128]{3,2,1,0:T(8,128)} %bitcast.13, s32[4,32]{1,0:T(4,128)} %bitcast.16, s32[4,32]{1,0:T(4,128)} %bitcast.17), custom_call_target="tpu_custom_call" | custom-call | tf_op jit(solution)/shard_map/pallas_call | solution.py:601
  23.5 0.9 %shard_map.69 = (f32[80,1280]{1,0:T(8,128)}, f32[288,384]{1,0:T(8,128)}) custom-call(f32[80,1280]{1,0:T(8,128)S(1)} %get-tuple-element.6.cond, f32[288,384]{1,0:T(8,128)S(1)} %get-tuple-element.7.coarse), custom_call_target="tpu_custom_call" | custom-call | tf_op jit(solution)/shard_map/pallas_call | solution.py:658
